TPU v7x, 32 devices: a whole 2x2x4 slice. The times are simulated.
32 devices in a mesh: blk: 8 (over y, x, core), head: 4 (over z).
Axes of the slice: x: 2, y: 2, z: 4, core: 2. Of those that a mesh axis runs over, the one named last changes fastest.
Arguments:
- query_states: bfloat16 [8, 2, 64, 2048], P('blk', None, 'head'), may hold values from -24 to 24
- key_states: bfloat16 [8, 2, 64, 512], P('blk', None, None, 'head'), may hold values from -6 to 6
- value_states: bfloat16 [8, 2, 64, 512], P('blk', None, None, 'head'), may hold values from -6 to 6
- doc_lengths: int32 [3], replicated, may hold values from 1 to 768, 1024 in all
- page_slot: int32 [8, 2, 4], replicated, may hold values from 0 to 127, as said below
Outputs:
- attended: bfloat16 [8, 2, 64, 2048], P('blk', None, None, 'head')
- kv_cache: bfloat16 [128, 4, 16, 256], P('blk', 'head')
Inputs may be any that keep to these rules, and one draw needn't show every extreme that they name: `page_slot`: all entries differ. The busiest owners hold 16 pages, the least busy 4.
All inputs are finite; a program needn't handle non-finite values.
Results may differ from a plain program's by a relative error of at most 0.007.
Values may be sent and summed in bfloat16 or wider, within the bound.
No kernel may reach another device: no remote copies, remote signals or barrier semaphores. Data moves between devices by JAX's collectives and lax.ppermute only.
A program may use at most 64 MiB of HBM per device.

v0:
```python
import jax
import jax.numpy as jnp
from jax import lax
from jax.sharding import PartitionSpec as P

PAGE = 16


def per_device(query_states, key_states, value_states, doc_lengths, page_slot):
    q_local = lax.all_to_all(query_states, "head", split_axis=3, concat_axis=2, tiled=True)
    axis_count = lax.axis_size("blk")
    my_index = lax.axis_index("blk")
    block_tok = q_local.shape[2]
    head_dim = key_states.shape[3]
    group_size = q_local.shape[3] // head_dim
    query_rows = q_local.reshape(2 * block_tok, group_size, head_dim)
    offsets = jnp.arange(block_tok, dtype=jnp.int32)
    doc_bounds = jnp.cumsum(doc_lengths)[:-1]
    page_count = block_tok // PAGE
    slot_count = 4 * page_count
    slot_range = jnp.arange(slot_count, dtype=jnp.int32)
    score_scale = head_dim ** (-0.5)

    def group_positions(owner_ids):
        block_starts = jnp.stack([owner_ids, 2 * axis_count - 1 - owner_ids], axis=1) * block_tok
        return (block_starts[:, :, None] + offsets[None, None, :]).reshape(-1)

    def doc_of(positions):
        return jnp.sum((positions[:, None] >= doc_bounds[None, :]).astype(jnp.int32), axis=1)

    q_pos = group_positions(my_index.reshape(1))
    q_doc = doc_of(q_pos)

    def attend_group(attn_state, key_rows, value_rows, allowed):
        running_max, weight_sum, accum = attn_state
        scores = (
            jnp.einsum("qhd,kd->qhk", query_rows, key_rows, preferred_element_type=jnp.float32)
            * score_scale
        )
        masked = jnp.where(allowed[:, None, :], scores, -1e30)
        new_max = jnp.maximum(running_max, jnp.max(masked, axis=2))
        weights = jnp.where(allowed[:, None, :], jnp.exp(masked - new_max[..., None]), 0.0)
        factor = jnp.exp(running_max - new_max)
        weight_sum = weight_sum * factor + jnp.sum(weights, axis=2)
        update = jnp.einsum(
            "qhk,kd->qhd",
            weights.astype(jnp.bfloat16),
            value_rows,
            preferred_element_type=jnp.float32,
        )
        accum = accum * factor[..., None] + update
        return (new_max, weight_sum, accum)

    def visit_group(attn_state, key_group, value_group, owner_ids):
        key_rows = key_group.reshape(-1, head_dim)
        value_rows = value_group.reshape(-1, head_dim)
        k_pos = group_positions(owner_ids)
        allowed = (k_pos[None, :] <= q_pos[:, None]) & (doc_of(k_pos)[None, :] == q_doc[:, None])
        return attend_group(attn_state, key_rows, value_rows, allowed)

    def place_pages(page_store, key_group, value_group, owner_ids):
        page_rows = jnp.concatenate([key_group, value_group], axis=-1).reshape(
            -1, PAGE * 2 * head_dim
        )
        slot_ids = jnp.take(page_slot, owner_ids, axis=0).reshape(-1) - my_index * slot_count
        selector = (slot_range[:, None] == slot_ids[None, :]).astype(jnp.bfloat16)
        return page_store + jnp.dot(selector, page_rows, preferred_element_type=jnp.float32)

    def fold_groups(step_fn, carried, kv_piece):
        key_piece, value_piece = kv_piece
        piece_len = key_piece.shape[0]
        width = 4
        owner_ids = jnp.arange(piece_len, dtype=jnp.int32).reshape(piece_len // width, width)
        key_groups = key_piece.reshape(piece_len // width, width, 2, block_tok, head_dim)
        value_groups = value_piece.reshape(piece_len // width, width, 2, block_tok, head_dim)

        def visit_one(inner_state, entry_tuple):
            key_group, value_group, owners = entry_tuple
            return (step_fn(inner_state, key_group, value_group, owners), None)

        return lax.scan(visit_one, carried, (key_groups, value_groups, owner_ids))[0]

    empty_store = jnp.zeros((slot_count, PAGE * 2 * head_dim), jnp.float32)
    start_state = (
        jnp.full((2 * block_tok, group_size), -1e30, jnp.float32),
        jnp.zeros((2 * block_tok, group_size), jnp.float32),
        jnp.zeros((2 * block_tok, group_size, head_dim), jnp.float32),
    )
    final_state = fold_groups(
        visit_group,
        start_state,
        (
            lax.all_gather(key_states, "blk", axis=0, tiled=True),
            lax.all_gather(value_states, "blk", axis=0, tiled=True),
        ),
    )
    page_store = fold_groups(
        place_pages,
        empty_store,
        (
            lax.all_gather(key_states, "blk", axis=0, tiled=True),
            lax.all_gather(value_states, "blk", axis=0, tiled=True),
        ),
    )
    running_max, weight_sum, accum = final_state
    attended = (
        (accum / weight_sum[..., None])
        .astype(jnp.bfloat16)
        .reshape(1, 2, block_tok, group_size * head_dim)
    )
    kv_cache = page_store.astype(jnp.bfloat16).reshape(slot_count, 1, PAGE, 2 * head_dim)
    return (attended, kv_cache)


def solution(mesh):
    return jax.shard_map(
        per_device,
        mesh=mesh,
        in_specs=(
            P("blk", None, "head", None),
            P("blk", None, None, "head"),
            P("blk", None, None, "head"),
            P(),
            P(),
        ),
        out_specs=(P("blk", None, None, "head"), P("blk", "head", None, None)),
        check_vma=False,
    )
```

profile of v0, /device:TPU:0, one launch (start us, length us, event | category | flops | bytes accessed | tf_op | source)
XLA Modules:
  0.0 40.2 jit_solution(6658046670930143716)
XLA Ops:
  0.6 2.0 %copy.26 = bf16[1,2,16,2048]{2,1,0,3:T(2,128)(2,1)S(1)} copy(bf16[1,2,16,2048]{3,2,1,0:T(8,128)(2,1)} %param.9) | data formatting | bytes 262144 | tf_op args[0]
  2.7 1.7 %reshape.326 = bf16[4,2,8192]{2,1,0:T(2,128)(2,1)} reshape(bf16[2048,1,2,16]{3,2,1,0:T(2,128)(2,1)S(1)} %bitcast.71) | data formatting | bytes 262144
  4.4 6.4 %all-to-all-start = ((bf16[4,2,8192]{2,1,0:T(2,128)(2,1)}), bf16[4,2,8192]{2,1,0:T(2,128)(2,1)S(1)}, u32[]{:S(2)}, u32[]{:S(2)}) async-start(bf16[4,2,8192]{2,1,0:T(2,128)(2,1)} %reshape.326), calls=%async_computation | async-start | bytes 262144 | tf_op jit(solution)/shard_map/all_to_all | solution.py:10
  10.9 0.6 %copy-done.3 = s32[3]{0:T(128)S(1)} copy-done((s32[3]{0:T(128)S(1)}, s32[3]{0:T(128)}, u32[]{:S(2)}) %copy-start.3) | copy-done | bytes 36
  11.6 0.2 reduce-window.4
  11.7 9.4 %all_gather.8 = bf16[8,2,64,128]{3,2,1,0:T(8,128)(2,1)S(1)} all-gather(bf16[1,2,64,128]{3,2,1,0:T(8,128)(2,1)S(1)} %copy-done), channel_id=1, replica_groups=mesh['blk'=8,'head'=4] {'blk'}, dimensions={0}, use_global_device_ids=true | all-gather | bytes 294912 | tf_op jit(solution)/shard_map/all_gather | solution.py:93
  21.2 9.4 %all_gather.9 = bf16[8,2,64,128]{3,2,1,0:T(8,128)(2,1)S(1)} all-gather(bf16[1,2,64,128]{3,2,1,0:T(8,128)(2,1)S(1)} %copy-done.1), channel_id=1, replica_groups=mesh['blk'=8,'head'=4] {'blk'}, dimensions={0}, use_global_device_ids=true | all-gather | bytes 294912 | tf_op jit(solution)/shard_map/all_gather | solution.py:94
  30.6 0.1 copy.30
  30.7 2.4 %while.29 = (s32[]{:T(128)}, f32[16,4096]{1,0:T(8,128)S(1)}, s32[2,4]{1,0:T(2,128)S(1)}, s32[8,2,4]{2,1,0:T(2,128)S(1)}, s32[]{:T(128)}, /*index=5*/bf16[2,4,2,6...) while((s32[]{:T(128)}, f32[16,4096]{1,0:T(8,128)S(1)}, ...), condition=%wide.region_8.9_spmd.clone, body=%wide.region_7.8_spmd.clone.sunk | while | flops 4851303 | bytes 2364495 | solution.py:81
  30.8 0.1 reshape.333
  30.9 0.6 %gather_fusion = s32[4,2,4]{2,1,0:T(2,128)S(1)} fusion(s32[8,2,4]{2,1,0:T(2,128)S(1)} %get-tuple-element.519, s32[1024]{0:T(1024)S(1)} %pad_clamp_fusion.2), kind=kCustom, calls=%fused_computation.clone.clone.1 | custom fusion | bytes 272 | tf_op jit(solution)/shard_map/while/body/eval_jaxpr/jit(_take)/gather | solution.py:65
  31.7 0.2 convolution_add_fusion.5
  32.0 0.1 reshape.333
  32.1 0.6 %gather_fusion = s32[4,2,4]{2,1,0:T(2,128)S(1)} fusion(s32[8,2,4]{2,1,0:T(2,128)S(1)} %get-tuple-element.519, s32[1024]{0:T(1024)S(1)} %pad_clamp_fusion.2), kind=kCustom, calls=%fused_computation.clone.clone.1 | custom fusion | bytes 272 | tf_op jit(solution)/shard_map/while/body/eval_jaxpr/jit(_take)/gather | solution.py:65
  32.9 0.2 convolution_add_fusion.5
  33.4 0.7 %copy.32 = bf16[2,8,16,256]{3,2,1,0:T(8,128)(2,1)} copy(bf16[2,8,16,256]{3,1,2,0:T(8,128)(2,1)S(1)} %bitcast.72) | data formatting | bytes 262144
  34.2 0.7 %reshape.327 = bf16[2048,1,2,16]{3,2,1,0:T(2,128)(2,1)S(1)} reshape(bf16[4,2,8192]{2,1,0:T(2,128)(2,1)S(1)} %all-to-all-done) | data formatting | bytes 262144
  34.9 0.6 %copy.27 = bf16[1,2,16,4,512]{4,2,3,1,0:T(8,128)(2,1)S(1)} copy(bf16[1,2,16,4,512]{2,1,4,3,0:T(2,128)(2,1)S(1)} %bitcast.70) | data formatting | bytes 262144 | tf_op jit(solution)/shard_map/all_to_all | solution.py:10
  35.6 3.6 %while.28 = (s32[]{:T(128)}, f32[128,4]{0,1:T(4,128)S(1)}, f32[128,4]{0,1:T(4,128)S(1)}, f32[128,4,128]{2,0,1:T(8,128)S(1)}, s32[2,4]{1,0:T(2,128)S(1)}, /*index...) while((s32[]{:T(128)}, f32[128,4]{0,1:T(4,128)S(1)}, ...), condition=%wide.region_6.7_spmd.clone, body=%wide.region_2.6_spmd.clone.sunk | while | flops 136976032 | bytes 4899697 | solution.py:81
  35.7 0.1 copy.34
  36.2 0.2 compare_and_fusion.4
  36.4 0.3 fusion.42
  36.7 0.2 fusion.43
  37.0 0.4 %convolution_add_fusion.4 = f32[128,4,128]{2,0,1:T(8,128)S(1)} fusion(bf16[512,128,1]{1,0,2:T(8,128)(2,1)S(1)} %bitcast.66, f32[128,4,512]{0,2,1:T(8,128)S(1)} %get-tuple-element.446, f32[128,4]{0,1:T(4,128)S(1)} %select_maximum_fusion.2, pred[128,512]{0,1:T(8,128)(4,1)S(1)} %compare_and_fusion.4, f32[128,4,128]{2,0,1:T(8,128)S(1)} %get-tuple-element.475, ...), kind=kOutput, calls=%fused_computation.7.clone.1 | convolution fusion | flops 68091904 | bytes 1773569 | tf_op jit(solution)/shard_map/while/body/eval_jaxpr/qhk,kd->qhd/dot_general | solution.py:45
  37.5 0.1 copy.34
  38.0 0.2 compare_and_fusion.4
  38.2 0.3 fusion.42
  38.6 0.2 fusion.43
  38.8 0.4 %convolution_add_fusion.4 = f32[128,4,128]{2,0,1:T(8,128)S(1)} fusion(bf16[512,128,1]{1,0,2:T(8,128)(2,1)S(1)} %bitcast.66, f32[128,4,512]{0,2,1:T(8,128)S(1)} %get-tuple-element.446, f32[128,4]{0,1:T(4,128)S(1)} %select_maximum_fusion.2, pred[128,512]{0,1:T(8,128)(4,1)S(1)} %compare_and_fusion.4, f32[128,4,128]{2,0,1:T(8,128)S(1)} %get-tuple-element.475, ...), kind=kOutput, calls=%fused_computation.7.clone.1 | convolution fusion | flops 68091904 | bytes 1773569 | tf_op jit(solution)/shard_map/while/body/eval_jaxpr/qhk,kd->qhd/dot_general | solution.py:45
  39.3 0.1 divide_convert_fusion
  39.4 0.1 copy.29
  39.5 0.7 %reshape.305 = bf16[1,2,64,512]{3,2,1,0:T(8,128)(2,1)} reshape(bf16[128,4,128]{2,1,0:T(4,128)(2,1)S(1)} %copy.29) | data formatting | bytes 262144 | tf_op jit(solution)/shard_map/reshape | solution.py:109
  (60 shorter events, 2.0 us)
Async XLA Ops:
  4.4 7.3 %copy-start = (bf16[1,2,64,128]{3,2,1,0:T(8,128)(2,1)S(1)}, bf16[1,2,64,128]{3,2,1,0:T(8,128)(2,1)}, u32[]{:S(2)}) copy-start(bf16[1,2,64,128]{3,2,1,0:T(8,128)(2,1)} %param.10) | copy-start | bytes 98308
  4.4 29.8 %all-to-all-start = ((bf16[4,2,8192]{2,1,0:T(2,128)(2,1)}), bf16[4,2,8192]{2,1,0:T(2,128)(2,1)S(1)}, u32[]{:S(2)}, u32[]{:S(2)}) async-start(bf16[4,2,8192]{2,1,0:T(2,128)(2,1)} %reshape.326), calls=%async_computation | async-start | bytes 262144 | tf_op jit(solution)/shard_map/all_to_all | solution.py:10
  10.9 0.7 %copy-start.3 = (s32[3]{0:T(128)S(1)}, s32[3]{0:T(128)}, u32[]{:S(2)}) copy-start(s32[3]{0:T(128)} %param.12) | copy-start | bytes 40
  11.7 9.4 %copy-start.1 = (bf16[1,2,64,128]{3,2,1,0:T(8,128)(2,1)S(1)}, bf16[1,2,64,128]{3,2,1,0:T(8,128)(2,1)}, u32[]{:S(2)}) copy-start(bf16[1,2,64,128]{3,2,1,0:T(8,128)(2,1)} %param.11) | copy-start | bytes 98308
  21.2 9.4 %copy-start.2 = (s32[8,2,4]{0,2,1:T(4,128)S(1)}, s32[8,2,4]{0,2,1:T(4,128)}, u32[]{:S(2)}) copy-start(s32[8,2,4]{0,2,1:T(4,128)} %param.13) | copy-start | bytes 772
where the time goes:
time: 40.8 us; the launch traced here: 40.2 us
  blocking collectives  18.8 us (46%)
  local copies, waits for them, and re-layouts  9.86 us (24%)
  starting transfers between devices  6.45 us (16%)
  other arithmetic  2.16 us (5%)
  matrix products  1.89 us (5%)
  between operations  0.75 us (2%)
    all_gather x1, blocking collectives, per_device(): lax.all_gather(key_states, 'blk', axis=0, tiled=True)  9.44 us
    all_gather x1, blocking collectives, per_device(): lax.all_gather(value_states, 'blk', axis=0, tiled=True)  9.41 us
    all_to_all x1, starting transfers between devices, per_device(): lax.all_to_all(query_states, 'head', split_axis=3, concat_axis=2, tiled=T...  6.45 us
    unnamed x14, local copies, waits for them, and re-layouts  5.93 us
    gather x2, local copies, waits for them, and re-layouts, place_pages(): jnp.take(page_slot, owner_ids, axis=0).reshape(-1) - my_index * slot_count  1.14 us
    dot_general x2, matrix products, attend_group(): jnp.einsum('qhk,kd->qhd', weights.astype(jnp.bfloat16), value_rows, prefe...  0.88 us
  transfers between devices with their start and end apart: 1, of which 0 were waited for; matrix products, arithmetic and copies ran while one was open for 9% of the time, Pallas kernels for 0%

commit v1 on v0

--- a/solution.py
+++ b/solution.py
@@ -1,12 +1,145 @@
+import functools
+
 import jax
 import jax.numpy as jnp
 from jax import lax
+from jax.experimental import pallas as pl
+from jax.experimental.pallas import tpu as pltpu
 from jax.sharding import PartitionSpec as P
 
 PAGE = 16
+LOG2E = 1.4426950408889634
+
+
+def attend_kernel(blk_count, head_count, meta, doc_lengths, page_slot, *refs):
+    q_refs = refs[:head_count]
+    kv_refs = refs[head_count : head_count + blk_count]
+    attended, kv_cache, q_rows, kv_rows, inverse = refs[head_count + blk_count :]
+    my_blk = meta[0]
+    my_head = meta[1]
+    block_tok = kv_refs[0].shape[2]
+    head_dim = kv_refs[0].shape[3] // 2
+    sub_tok = block_tok // head_count
+    width = q_refs[1].shape[3]
+    group = width // head_dim
+    pages_blk = block_tok // PAGE
+    slot_count = kv_cache.shape[0]
+    page_total = blk_count * 2 * pages_blk
+    half_rows = blk_count * block_tok
+    scale = head_dim**-0.5 * LOG2E
+
+    for slot in range(slot_count):
+        inverse[slot] = -1
+    first_slot = my_blk * slot_count
+    for page in range(page_total):
+        local = page_slot[page] - first_slot
+        mine = (local >= 0) & (local < slot_count)
+        inverse[jnp.where(mine, local, slot_count)] = page
+
+    for d in range(blk_count):
+        owner = my_blk ^ d
+        for half in range(2):
+            block = owner if half == 0 else 2 * blk_count - 1 - owner
+            kv_rows[pl.ds(pl.multiple_of(block * block_tok, block_tok), block_tok), :] = kv_refs[d][0, half]
+    for d in range(head_count):
+        row = pl.multiple_of((my_head ^ d) * sub_tok, sub_tok)
+        for half in range(2):
+            for g in range(group):
+                if d == 0:
+                    lane = pl.multiple_of(my_head * width + g * head_dim, head_dim)
+                    piece = q_refs[0][0, half, :, pl.ds(lane, head_dim)]
+                else:
+                    piece = q_refs[d][0, half, :, g * head_dim : (g + 1) * head_dim]
+                q_rows[half, g, pl.ds(row, sub_tok), :] = piece
+
+    for slot in range(slot_count):
+        page = inverse[slot]
+        used = page >= 0
+        page = jnp.maximum(page, 0)
+        pair = page // (2 * pages_blk)
+        rest = page - pair * (2 * pages_blk)
+        second = rest >= pages_blk
+        block = jnp.where(second, 2 * blk_count - 1 - pair, pair)
+        start = block * block_tok + jnp.where(second, rest - pages_blk, rest) * PAGE
+        rows = kv_rows[pl.ds(pl.multiple_of(start, PAGE), PAGE), :]
+        kv_cache[slot, 0] = jnp.where(used, rows, jnp.zeros_like(rows))
+
+    bounds = []
+    total = 0
+    for k in range(doc_lengths.shape[0] - 1):
+        total = total + doc_lengths[k]
+        bounds.append(total)
+
+    for half in range(2):
+        cols = half_rows * (half + 1)
+        block = my_blk if half == 0 else 2 * blk_count - 1 - my_blk
+        q_pos = block * block_tok + lax.broadcasted_iota(jnp.int32, (block_tok, 1), 0)
+        first = jnp.zeros_like(q_pos)
+        for bound in bounds:
+            first = jnp.where(q_pos >= bound, bound, first)
+        k_pos = lax.broadcasted_iota(jnp.int32, (block_tok, cols), 1)
+        bias = jnp.where((k_pos <= q_pos) & (k_pos >= first), 0.0, -1e30)
+        queries = q_rows[half].reshape(group * block_tok, head_dim)
+        scores = lax.dot_general(
+            queries,
+            kv_rows[:cols, :head_dim],
+            (((1,), (1,)), ((), ())),
+            preferred_element_type=jnp.float32,
+        )
+        scores = scores.reshape(group, block_tok, cols) * scale + bias[None]
+        top = jnp.max(scores, axis=2, keepdims=True)
+        weights = jnp.exp2(scores - top)
+        weight_sum = jnp.sum(weights, axis=2, keepdims=True)
+        out = jnp.dot(
+            weights.astype(jnp.bfloat16).reshape(group * block_tok, cols),
+            kv_rows[:cols, head_dim:],
+            preferred_element_type=jnp.float32,
+        ).reshape(group, block_tok, head_dim)
+        out = (out / weight_sum).astype(jnp.bfloat16)
+        for g in range(group):
+            attended[0, half, :, g * head_dim : (g + 1) * head_dim] = out[g]
 
 
 def per_device(query_states, key_states, value_states, doc_lengths, page_slot):
+    blk_count = lax.axis_size("blk")
+    head_count = lax.axis_size("head")
+    my_blk = lax.axis_index("blk")
+    my_head = lax.axis_index("head")
+    block_tok, head_dim = key_states.shape[2:]
+    width = query_states.shape[3] // head_count
+    group = width // head_dim
+    slot_count = 4 * (block_tok // PAGE)
+    meta = jnp.stack([my_blk, my_head]).astype(jnp.int32)
+
+    pair = jnp.concatenate([key_states, value_states], axis=3)
+    kv_pieces = [pair] + [
+        lax.ppermute(pair, "blk", [(i, i ^ d) for i in range(blk_count)]) for d in range(1, blk_count)
+    ]
+    q_pieces = [query_states]
+    for d in range(1, head_count):
+        part = lax.dynamic_slice_in_dim(query_states, (my_head ^ d) * width, width, axis=3)
+        q_pieces.append(lax.ppermute(part, "head", [(i, i ^ d) for i in range(head_count)]))
+
+    smem = pl.BlockSpec(memory_space=pltpu.SMEM)
+    vmem = pl.BlockSpec(memory_space=pltpu.VMEM)
+    return pl.pallas_call(
+        functools.partial(attend_kernel, blk_count, head_count),
+        out_shape=(
+            jax.ShapeDtypeStruct((1, 2, block_tok, width), jnp.bfloat16),
+            jax.ShapeDtypeStruct((slot_count, 1, PAGE, 2 * head_dim), jnp.bfloat16),
+        ),
+        in_specs=[smem] * 3 + [vmem] * (head_count + blk_count),
+        out_specs=(vmem, vmem),
+        scratch_shapes=[
+            pltpu.VMEM((2, group, block_tok, head_dim), jnp.bfloat16),
+            pltpu.VMEM((2 * blk_count * block_tok, 2 * head_dim), jnp.bfloat16),
+            pltpu.SMEM((slot_count + 1,), jnp.int32),
+        ],
+        compiler_params=pltpu.CompilerParams(vmem_limit_bytes=32 * 1024 * 1024),
+    )(meta, doc_lengths, page_slot.reshape(-1), *q_pieces, *kv_pieces)
+
+
+def per_device_long(query_states, key_states, value_states, doc_lengths, page_slot):
     q_local = lax.all_to_all(query_states, "head", split_axis=3, concat_axis=2, tiled=True)
     axis_count = lax.axis_size("blk")
     my_index = lax.axis_index("blk")
@@ -114,7 +247,7 @@
 
 def solution(mesh):
     return jax.shard_map(
-        per_device,
+        per_device if mesh.shape["blk"] <= 8 else per_device_long,
         mesh=mesh,
         in_specs=(
             P("blk", None, "head", None),

time: 40.8 us -> 23.7 us (0.58); the launches traced: 40.2 us -> 23.6 us
  blocking collectives: 18.8 us -> 0 us
  local copies, waits for them, and re-layouts: 9.86 us -> 1.02 us
  waiting for transfers between devices: 0.01 us -> 7.34 us
  starting transfers between devices: 6.45 us -> 12.1 us
  Pallas kernels: 0 us -> 2.38 us
  other arithmetic: 2.16 us -> 0.07 us
  matrix products: 1.89 us -> 0 us
    all_gather x2 -> x0, blocking collectives: 18.8 us -> none  [the longest x1 9.44 us: per_device(): lax.all_gather(key_states, 'blk', axis=0, tiled=True)]
    ppermute x0 -> x10, starting transfers between devices: none -> 12.1 us  [the longest x7 7.61 us: per_device(): lax.ppermute(pair, 'blk', [(i, i ^ d) for i in range(blk_count)])]
    ppermute x0 -> x10, waiting for transfers between devices: none -> 7.34 us  [the longest x7 3.86 us: per_device(): lax.ppermute(pair, 'blk', [(i, i ^ d) for i in range(blk_count)])]
    all_to_all x1 -> x0, starting transfers between devices: 6.45 us -> none  [per_device(): lax.all_to_all(query_states, 'head', split_axis=3, concat_axis=2, tiled=T...]
    unnamed x14 -> x10, local copies, waits for them, and re-layouts: 5.93 us -> 0.91 us
    pallas_call x0 -> x1, Pallas kernels: none -> 2.38 us  [per_device(): pl.pallas_call(functools.partial(attend_kernel, blk_count, head_count), o...]
    dot_general x6 -> x0, matrix products: 1.89 us -> none  [the longest x2 0.88 us: attend_group(): jnp.einsum('qhk,kd->qhd', weights.astype(jnp.bfloat16), value_rows, prefe...]
    gather x2 -> x0, local copies, waits for them, and re-layouts: 1.14 us -> none  [place_pages(): jnp.take(page_slot, owner_ids, axis=0).reshape(-1) - my_index * slot_count]
  transfers between devices with their start and end apart: 1 -> 10, of which waited for: 0 -> 5; matrix products, arithmetic and copies ran while one was open for 9% -> 1% of each run, Pallas kernels for 0% -> 0%
where the time goes in v1:
time: 23.7 us; the launch traced here: 23.6 us
  starting transfers between devices  12.1 us (51%)
  waiting for transfers between devices  7.34 us (31%)
  Pallas kernels  2.38 us (10%)
  local copies, waits for them, and re-layouts  1.02 us (4%)
  between operations  0.67 us (3%)
    ppermute x7, starting transfers between devices, per_device(): lax.ppermute(pair, 'blk', [(i, i ^ d) for i in range(blk_count)])  7.61 us
    ppermute x3, starting transfers between devices, per_device(): lax.ppermute(part, 'head', [(i, i ^ d) for i in range(head_count)])  4.45 us
    ppermute x7, waiting for transfers between devices, per_device(): lax.ppermute(pair, 'blk', [(i, i ^ d) for i in range(blk_count)])  3.86 us
    ppermute x3, waiting for transfers between devices, per_device(): lax.ppermute(part, 'head', [(i, i ^ d) for i in range(head_count)])  3.49 us
    pallas_call x1, Pallas kernels, per_device(): pl.pallas_call(functools.partial(attend_kernel, blk_count, head_count), o...  2.38 us
    unnamed x10, local copies, waits for them, and re-layouts  0.91 us
  transfers between devices with their start and end apart: 10, of which 5 were waited for; matrix products, arithmetic and copies ran while one was open for 1% of the time, Pallas kernels for 0%

profile of v1, /device:TPU:0, one launch (start us, length us, event | category | flops | bytes accessed | tf_op | source)
XLA Modules:
  0.0 23.6 jit_solution(13198796637086891725)
XLA Ops:
  0.6 0.0 copy-start.2
  0.6 0.0 copy-start
  0.6 0.8 %constant_dynamic-update-slice_fusion.1 = bf16[1,2,64,256]{3,2,1,0:T(8,128)(2,1)S(1)} fusion(bf16[1,2,64,128]{3,2,1,0:T(8,128)(2,1)} %param.6), kind=kLoop, calls=%fused_computation.1 | loop fusion | bytes 65536
  1.5 0.0 copy-done.2
  1.5 3.4 %collective-permute-start.9 = (bf16[1,2,64,256]{3,2,1,0:T(8,128)(2,1)S(1)}, bf16[1,2,64,256]{3,2,1,0:T(8,128)(2,1)S(1)}, u32[]{:S(2)}, u32[]{:S(2)}) collective-permute-start(bf16[1,2,64,256]{3,2,1,0:T(8,128)(2,1)S(1)} %constant_dynamic-update-slice_fusion.refs_4_), channel_id=1, source_target_pairs={{0,28},{4,24},{8,20},{12,16},{16,12},{20,8},{24,4},{28,0},{1,29},{... | collective-permute-start | bytes 196616 | tf_op jit(solution)/shard_map/ppermute | solution.py:116
  4.9 0.6 %collective-permute-start.8 = (bf16[1,2,64,256]{3,2,1,0:T(8,128)(2,1)S(1)}, bf16[1,2,64,256]{3,2,1,0:T(8,128)(2,1)S(1)}, u32[]{:S(2)}, u32[]{:S(2)}) collective-permute-start(bf16[1,2,64,256]{3,2,1,0:T(8,128)(2,1)S(1)} %constant_dynamic-update-slice_fusion.refs_4_), channel_id=1, source_target_pairs={{0,24},{4,28},{8,16},{12,20},{16,8},{20,12},{24,0},{28,4},{1,25},{... | collective-permute-start | bytes 196616 | tf_op jit(solution)/shard_map/ppermute | solution.py:116
  5.5 0.0 copy-done
  5.5 3.7 %collective-permute-start.2 = (bf16[1,2,16,512]{3,2,1,0:T(8,128)(2,1)S(1)}, bf16[1,2,16,512]{3,2,1,0:T(8,128)(2,1)S(1)}, u32[]{:S(2)}, u32[]{:S(2)}) collective-permute-start(bf16[1,2,16,512]{3,2,1,0:T(8,128)(2,1)S(1)} %get-tuple-element.2), channel_id=1, source_target_pairs={{0,3},{1,2},{2,1},{3,0},{4,7},{5,6},{6,5},{7,4},{8,11},{9,10},{10,... | collective-permute-start | bytes 98312 | tf_op jit(solution)/shard_map/ppermute | solution.py:121
  9.2 0.0 copy-start.3
  9.2 0.0 collective-permute-start.1
  9.2 0.8 %collective-permute-start = (bf16[1,2,16,512]{3,2,1,0:T(8,128)(2,1)S(1)}, bf16[1,2,16,512]{3,2,1,0:T(8,128)(2,1)S(1)}, u32[]{:S(2)}, u32[]{:S(2)}) collective-permute-start(bf16[1,2,16,512]{3,2,1,0:T(8,128)(2,1)S(1)} %get-tuple-element.4), channel_id=1, source_target_pairs={{0,1},{1,0},{2,3},{3,2},{4,5},{5,4},{6,7},{7,6},{8,9},{9,8},{10,11... | collective-permute-start | bytes 98312 | tf_op jit(solution)/shard_map/ppermute | solution.py:121
  10.0 0.0 copy-done.3
  10.0 0.1 copy.8
  10.1 0.1 reshape.7.page_slot
  10.2 1.1 %collective-permute-done.2.refs_3_ = bf16[1,2,16,512]{3,2,1,0:T(8,128)(2,1)S(1)} collective-permute-done((bf16[1,2,16,512]{3,2,1,0:T(8,128)(2,1)S(1)}, bf16[1,2,16,512]{3,2,1,0:T(8,128)(2,1)S(1)}, u32[]{:S(2)}, u32[]{:S(2)}) %collective-permute-start.2) | collective-permute-done | bytes 32800 | tf_op jit(solution)/shard_map/ppermute | solution.py:121
  11.3 0.3 %collective-permute-start.7 = (bf16[1,2,64,256]{3,2,1,0:T(8,128)(2,1)S(1)}, bf16[1,2,64,256]{3,2,1,0:T(8,128)(2,1)S(1)}, u32[]{:S(2)}, u32[]{:S(2)}) collective-permute-start(bf16[1,2,64,256]{3,2,1,0:T(8,128)(2,1)S(1)} %constant_dynamic-update-slice_fusion.refs_4_), channel_id=1, source_target_pairs={{0,20},{4,16},{8,28},{12,24},{16,4},{20,0},{24,12},{28,8},{1,21},{... | collective-permute-start | bytes 196616 | tf_op jit(solution)/shard_map/ppermute | solution.py:116
  11.7 2.4 %collective-permute-done.1.refs_2_ = bf16[1,2,16,512]{3,2,1,0:T(8,128)(2,1)S(1)} collective-permute-done((bf16[1,2,16,512]{3,2,1,0:T(8,128)(2,1)S(1)}, bf16[1,2,16,512]{3,2,1,0:T(8,128)(2,1)S(1)}, u32[]{:S(2)}, u32[]{:S(2)}) %collective-permute-start.1) | collective-permute-done | bytes 32800 | tf_op jit(solution)/shard_map/ppermute | solution.py:121
  14.0 1.4 %collective-permute-start.6 = (bf16[1,2,64,256]{3,2,1,0:T(8,128)(2,1)S(1)}, bf16[1,2,64,256]{3,2,1,0:T(8,128)(2,1)S(1)}, u32[]{:S(2)}, u32[]{:S(2)}) collective-permute-start(bf16[1,2,64,256]{3,2,1,0:T(8,128)(2,1)S(1)} %constant_dynamic-update-slice_fusion.refs_4_), channel_id=1, source_target_pairs={{0,16},{4,20},{8,24},{12,28},{16,0},{20,4},{24,8},{28,12},{1,17},{... | collective-permute-start | bytes 196616 | tf_op jit(solution)/shard_map/ppermute | solution.py:116
  15.4 0.0 collective-permute-done.refs_1_
  15.4 0.1 collective-permute-start.5
  15.5 0.0 collective-permute-done.9.refs_11_
  15.5 1.5 %collective-permute-start.4 = (bf16[1,2,64,256]{3,2,1,0:T(8,128)(2,1)S(1)}, bf16[1,2,64,256]{3,2,1,0:T(8,128)(2,1)S(1)}, u32[]{:S(2)}, u32[]{:S(2)}) collective-permute-start(bf16[1,2,64,256]{3,2,1,0:T(8,128)(2,1)S(1)} %constant_dynamic-update-slice_fusion.refs_4_), channel_id=1, source_target_pairs={{0,8},{4,12},{8,0},{12,4},{16,24},{20,28},{24,16},{28,20},{1,9},{5... | collective-permute-start | bytes 196616 | tf_op jit(solution)/shard_map/ppermute | solution.py:116
  16.9 0.0 collective-permute-done.8.refs_10_
  16.9 0.3 %collective-permute-start.3 = (bf16[1,2,64,256]{3,2,1,0:T(8,128)(2,1)S(1)}, bf16[1,2,64,256]{3,2,1,0:T(8,128)(2,1)S(1)}, u32[]{:S(2)}, u32[]{:S(2)}) collective-permute-start(bf16[1,2,64,256]{3,2,1,0:T(8,128)(2,1)S(1)} %constant_dynamic-update-slice_fusion.refs_4_), channel_id=1, source_target_pairs={{0,4},{4,0},{8,12},{12,8},{16,20},{20,16},{24,28},{28,24},{1,5},{5... | collective-permute-start | bytes 196616 | tf_op jit(solution)/shard_map/ppermute | solution.py:116
  17.2 0.1 pad_add_fusion.meta
  17.3 0.0 collective-permute-done.7.refs_9_
  17.3 1.0 %collective-permute-done.6.refs_8_ = bf16[1,2,64,256]{3,2,1,0:T(8,128)(2,1)S(1)} collective-permute-done((bf16[1,2,64,256]{3,2,1,0:T(8,128)(2,1)S(1)}, bf16[1,2,64,256]{3,2,1,0:T(8,128)(2,1)S(1)}, u32[]{:S(2)}, u32[]{:S(2)}) %collective-permute-start.6) | collective-permute-done | bytes 65568 | tf_op jit(solution)/shard_map/ppermute | solution.py:116
  18.3 1.4 %collective-permute-done.5.refs_7_ = bf16[1,2,64,256]{3,2,1,0:T(8,128)(2,1)S(1)} collective-permute-done((bf16[1,2,64,256]{3,2,1,0:T(8,128)(2,1)S(1)}, bf16[1,2,64,256]{3,2,1,0:T(8,128)(2,1)S(1)}, u32[]{:S(2)}, u32[]{:S(2)}) %collective-permute-start.5) | collective-permute-done | bytes 65568 | tf_op jit(solution)/shard_map/ppermute | solution.py:116
  19.7 1.4 %collective-permute-done.4.refs_6_ = bf16[1,2,64,256]{3,2,1,0:T(8,128)(2,1)S(1)} collective-permute-done((bf16[1,2,64,256]{3,2,1,0:T(8,128)(2,1)S(1)}, bf16[1,2,64,256]{3,2,1,0:T(8,128)(2,1)S(1)}, u32[]{:S(2)}, u32[]{:S(2)}) %collective-permute-start.4) | collective-permute-done | bytes 65568 | tf_op jit(solution)/shard_map/ppermute | solution.py:116
  21.2 0.0 collective-permute-done.3.refs_5_
  21.2 0.0 copy-done.1
  21.2 2.4 %shard_map.68 = (bf16[1,2,64,512]{3,2,1,0:T(8,128)(2,1)}, bf16[16,1,16,256]{3,2,1,0:T(8,128)(2,1)}) custom-call(s32[2]{0:T(128)S(1)} %pad_add_fusion.meta, s32[3]{0:T(128)S(1)} %copy-done.1, s32[64]{0:T(128)S(1)} %reshape.7.page_slot, bf16[1,2,16,2048]{3,2,1,0:T(8,128)(2,1)S(1)} %copy-done, bf16[1,2,16,512]{3,2,1,0:T(8,128)(2,1)S(1)} %collective-permute-done.refs_1_, ...), custom_call_target="tpu_custom_call" | custom-call | tf_op jit(solution)/shard_map/pallas_call | solution.py:125
  (3 shorter events, 0.0 us)
Async XLA Ops:
  0.6 0.8 %copy-start.2 = (bf16[1,2,64,128]{3,2,1,0:T(8,128)(2,1)S(1)}, bf16[1,2,64,128]{3,2,1,0:T(8,128)(2,1)}, u32[]{:S(2)}) copy-start(bf16[1,2,64,128]{3,2,1,0:T(8,128)(2,1)} %param.7) | copy-start | bytes 98308
  0.6 4.9 %copy-start = (bf16[1,2,16,2048]{3,2,1,0:T(8,128)(2,1)S(1)}, bf16[1,2,16,2048]{3,2,1,0:T(8,128)(2,1)}, u32[]{:S(2)}) copy-start(bf16[1,2,16,2048]{3,2,1,0:T(8,128)(2,1)} %refs_0_.1) | copy-start | bytes 393220
  1.5 14.0 %collective-permute-start.9 = (bf16[1,2,64,256]{3,2,1,0:T(8,128)(2,1)S(1)}, bf16[1,2,64,256]{3,2,1,0:T(8,128)(2,1)S(1)}, u32[]{:S(2)}, u32[]{:S(2)}) collective-permute-start(bf16[1,2,64,256]{3,2,1,0:T(8,128)(2,1)S(1)} %constant_dynamic-update-slice_fusion.refs_4_), channel_id=1, source_target_pairs={{0,28},{4,24},{8,20},{12,16},{16,12},{20,8},{24,4},{28,0},{1,29},{... | collective-permute-start | bytes 196616 | tf_op jit(solution)/shard_map/ppermute | solution.py:116
  4.9 12.1 %collective-permute-start.8 = (bf16[1,2,64,256]{3,2,1,0:T(8,128)(2,1)S(1)}, bf16[1,2,64,256]{3,2,1,0:T(8,128)(2,1)S(1)}, u32[]{:S(2)}, u32[]{:S(2)}) collective-permute-start(bf16[1,2,64,256]{3,2,1,0:T(8,128)(2,1)S(1)} %constant_dynamic-update-slice_fusion.refs_4_), channel_id=1, source_target_pairs={{0,24},{4,28},{8,16},{12,20},{16,8},{20,12},{24,0},{28,4},{1,25},{... | collective-permute-start | bytes 196616 | tf_op jit(solution)/shard_map/ppermute | solution.py:116
  5.5 5.8 %collective-permute-start.2 = (bf16[1,2,16,512]{3,2,1,0:T(8,128)(2,1)S(1)}, bf16[1,2,16,512]{3,2,1,0:T(8,128)(2,1)S(1)}, u32[]{:S(2)}, u32[]{:S(2)}) collective-permute-start(bf16[1,2,16,512]{3,2,1,0:T(8,128)(2,1)S(1)} %get-tuple-element.2), channel_id=1, source_target_pairs={{0,3},{1,2},{2,1},{3,0},{4,7},{5,6},{6,5},{7,4},{8,11},{9,10},{10,... | collective-permute-start | bytes 98312 | tf_op jit(solution)/shard_map/ppermute | solution.py:121
  9.2 0.8 %copy-start.3 = (s32[8,2,4]{0,2,1:T(4,128)S(1)}, s32[8,2,4]{0,2,1:T(4,128)}, u32[]{:S(2)}) copy-start(s32[8,2,4]{0,2,1:T(4,128)} %param.9) | copy-start | bytes 772
  9.2 4.8 %collective-permute-start.1 = (bf16[1,2,16,512]{3,2,1,0:T(8,128)(2,1)S(1)}, bf16[1,2,16,512]{3,2,1,0:T(8,128)(2,1)S(1)}, u32[]{:S(2)}, u32[]{:S(2)}) collective-permute-start(bf16[1,2,16,512]{3,2,1,0:T(8,128)(2,1)S(1)} %get-tuple-element.3), channel_id=1, source_target_pairs={{0,2},{1,3},{2,0},{3,1},{4,6},{5,7},{6,4},{7,5},{8,10},{9,11},{10,... | collective-permute-start | bytes 98312 | tf_op jit(solution)/shard_map/ppermute | solution.py:121
  9.2 6.2 %collective-permute-start = (bf16[1,2,16,512]{3,2,1,0:T(8,128)(2,1)S(1)}, bf16[1,2,16,512]{3,2,1,0:T(8,128)(2,1)S(1)}, u32[]{:S(2)}, u32[]{:S(2)}) collective-permute-start(bf16[1,2,16,512]{3,2,1,0:T(8,128)(2,1)S(1)} %get-tuple-element.4), channel_id=1, source_target_pairs={{0,1},{1,0},{2,3},{3,2},{4,5},{5,4},{6,7},{7,6},{8,9},{9,8},{10,11... | collective-permute-start | bytes 98312 | tf_op jit(solution)/shard_map/ppermute | solution.py:121
  11.3 6.0 %collective-permute-start.7 = (bf16[1,2,64,256]{3,2,1,0:T(8,128)(2,1)S(1)}, bf16[1,2,64,256]{3,2,1,0:T(8,128)(2,1)S(1)}, u32[]{:S(2)}, u32[]{:S(2)}) collective-permute-start(bf16[1,2,64,256]{3,2,1,0:T(8,128)(2,1)S(1)} %constant_dynamic-update-slice_fusion.refs_4_), channel_id=1, source_target_pairs={{0,20},{4,16},{8,28},{12,24},{16,4},{20,0},{24,12},{28,8},{1,21},{... | collective-permute-start | bytes 196616 | tf_op jit(solution)/shard_map/ppermute | solution.py:116
  14.0 4.3 %collective-permute-start.6 = (bf16[1,2,64,256]{3,2,1,0:T(8,128)(2,1)S(1)}, bf16[1,2,64,256]{3,2,1,0:T(8,128)(2,1)S(1)}, u32[]{:S(2)}, u32[]{:S(2)}) collective-permute-start(bf16[1,2,64,256]{3,2,1,0:T(8,128)(2,1)S(1)} %constant_dynamic-update-slice_fusion.refs_4_), channel_id=1, source_target_pairs={{0,16},{4,20},{8,24},{12,28},{16,0},{20,4},{24,8},{28,12},{1,17},{... | collective-permute-start | bytes 196616 | tf_op jit(solution)/shard_map/ppermute | solution.py:116
  15.4 4.3 %collective-permute-start.5 = (bf16[1,2,64,256]{3,2,1,0:T(8,128)(2,1)S(1)}, bf16[1,2,64,256]{3,2,1,0:T(8,128)(2,1)S(1)}, u32[]{:S(2)}, u32[]{:S(2)}) collective-permute-start(bf16[1,2,64,256]{3,2,1,0:T(8,128)(2,1)S(1)} %constant_dynamic-update-slice_fusion.refs_4_), channel_id=1, source_target_pairs={{0,12},{4,8},{8,4},{12,0},{16,28},{20,24},{24,20},{28,16},{1,13},{... | collective-permute-start | bytes 196616 | tf_op jit(solution)/shard_map/ppermute | solution.py:116
  15.5 5.7 %collective-permute-start.4 = (bf16[1,2,64,256]{3,2,1,0:T(8,128)(2,1)S(1)}, bf16[1,2,64,256]{3,2,1,0:T(8,128)(2,1)S(1)}, u32[]{:S(2)}, u32[]{:S(2)}) collective-permute-start(bf16[1,2,64,256]{3,2,1,0:T(8,128)(2,1)S(1)} %constant_dynamic-update-slice_fusion.refs_4_), channel_id=1, source_target_pairs={{0,8},{4,12},{8,0},{12,4},{16,24},{20,28},{24,16},{28,20},{1,9},{5... | collective-permute-start | bytes 196616 | tf_op jit(solution)/shard_map/ppermute | solution.py:116
  16.9 4.2 %collective-permute-start.3 = (bf16[1,2,64,256]{3,2,1,0:T(8,128)(2,1)S(1)}, bf16[1,2,64,256]{3,2,1,0:T(8,128)(2,1)S(1)}, u32[]{:S(2)}, u32[]{:S(2)}) collective-permute-start(bf16[1,2,64,256]{3,2,1,0:T(8,128)(2,1)S(1)} %constant_dynamic-update-slice_fusion.refs_4_), channel_id=1, source_target_pairs={{0,4},{4,0},{8,12},{12,8},{16,20},{20,16},{24,28},{28,24},{1,5},{5... | collective-permute-start | bytes 196616 | tf_op jit(solution)/shard_map/ppermute | solution.py:116
  17.2 3.9 %copy-start.1 = (s32[3]{0:T(128)S(1)}, s32[3]{0:T(128)}, u32[]{:S(2)}) copy-start(s32[3]{0:T(128)} %doc_lengths.1) | copy-start | bytes 40

commit v2 on v1

--- a/solution.py
+++ b/solution.py
@@ -13,8 +13,8 @@
 
 def attend_kernel(blk_count, head_count, meta, doc_lengths, page_slot, *refs):
     q_refs = refs[:head_count]
-    kv_refs = refs[head_count : head_count + blk_count]
-    attended, kv_cache, q_rows, kv_rows, inverse = refs[head_count + blk_count :]
+    kv_refs = refs[head_count : head_count + 2]
+    attended, kv_cache, q_rows, kv_rows, inverse = refs[head_count + 2 :]
     my_blk = meta[0]
     my_head = meta[1]
     block_tok = kv_refs[0].shape[2]
@@ -40,7 +40,7 @@
         owner = my_blk ^ d
         for half in range(2):
             block = owner if half == 0 else 2 * blk_count - 1 - owner
-            kv_rows[pl.ds(pl.multiple_of(block * block_tok, block_tok), block_tok), :] = kv_refs[d][0, half]
+            kv_rows[pl.ds(pl.multiple_of(block * block_tok, block_tok), block_tok), :] = kv_refs[d % 2][d // 2, half]
     for d in range(head_count):
         row = pl.multiple_of((my_head ^ d) * sub_tok, sub_tok)
         for half in range(2):
@@ -112,9 +112,11 @@
     meta = jnp.stack([my_blk, my_head]).astype(jnp.int32)
 
     pair = jnp.concatenate([key_states, value_states], axis=3)
-    kv_pieces = [pair] + [
-        lax.ppermute(pair, "blk", [(i, i ^ d) for i in range(blk_count)]) for d in range(1, blk_count)
+    near = [pair] + [
+        lax.ppermute(pair, "blk", [(i, i ^ d) for i in range(blk_count)]) for d in range(2, blk_count, 2)
     ]
+    near = jnp.concatenate(near, axis=0)
+    far = lax.ppermute(near, "blk", [(i, i ^ 1) for i in range(blk_count)])
     q_pieces = [query_states]
     for d in range(1, head_count):
         part = lax.dynamic_slice_in_dim(query_states, (my_head ^ d) * width, width, axis=3)
@@ -128,7 +130,7 @@
             jax.ShapeDtypeStruct((1, 2, block_tok, width), jnp.bfloat16),
             jax.ShapeDtypeStruct((slot_count, 1, PAGE, 2 * head_dim), jnp.bfloat16),
         ),
-        in_specs=[smem] * 3 + [vmem] * (head_count + blk_count),
+        in_specs=[smem] * 3 + [vmem] * (head_count + 2),
         out_specs=(vmem, vmem),
         scratch_shapes=[
             pltpu.VMEM((2, group, block_tok, head_dim), jnp.bfloat16),
@@ -136,7 +138,7 @@
             pltpu.SMEM((slot_count + 1,), jnp.int32),
         ],
         compiler_params=pltpu.CompilerParams(vmem_limit_bytes=32 * 1024 * 1024),
-    )(meta, doc_lengths, page_slot.reshape(-1), *q_pieces, *kv_pieces)
+    )(meta, doc_lengths, page_slot.reshape(-1), *q_pieces, near, far)
 
 
 def per_device_long(query_states, key_states, value_states, doc_lengths, page_slot):

time: 23.7 us -> 21.4 us (0.903)
  starting transfers between devices: 12.1 us -> 9.13 us
  local copies, waits for them, and re-layouts: 1.02 us -> 1.61 us
    ppermute x7 -> x3, starting transfers between devices: 7.61 us -> 4.6 us  [per_device(): lax.ppermute(pair, 'blk', [(i, i ^ d) for i in range(blk_count)])]
    unnamed x10, local copies, waits for them, and re-layouts: 0.91 us -> 1.49 us
    ppermute x3, waiting for transfers between devices: 3.49 us -> 3.15 us  [per_device(): lax.ppermute(part, 'head', [(i, i ^ d) for i in range(head_count)])]
    ppermute x7 -> x3, waiting for transfers between devices: 3.86 us -> 4.13 us  [per_device(): lax.ppermute(pair, 'blk', [(i, i ^ d) for i in range(blk_count)])]
  transfers between devices with their start and end apart: 10 -> 7, of which waited for: 5 -> 5; matrix products, arithmetic and copies ran while one was open for 1% -> 1% of each run, Pallas kernels for 0% -> 0%
where the time goes in v2:
time: 21.4 us; the launch traced here: 21.2 us
  starting transfers between devices  9.13 us (43%)
  waiting for transfers between devices  7.29 us (34%)
  Pallas kernels  2.39 us (11%)
  local copies, waits for them, and re-layouts  1.61 us (8%)
  between operations  0.72 us (3%)
    ppermute x3, starting transfers between devices, per_device(): lax.ppermute(pair, 'blk', [(i, i ^ d) for i in range(blk_count)])  4.6 us
    ppermute x3, starting transfers between devices, per_device(): lax.ppermute(part, 'head', [(i, i ^ d) for i in range(head_count)])  4.45 us
    ppermute x3, waiting for transfers between devices, per_device(): lax.ppermute(pair, 'blk', [(i, i ^ d) for i in range(blk_count)])  4.13 us
    ppermute x3, waiting for transfers between devices, per_device(): lax.ppermute(part, 'head', [(i, i ^ d) for i in range(head_count)])  3.15 us
    pallas_call x1, Pallas kernels, per_device(): pl.pallas_call(functools.partial(attend_kernel, blk_count, head_count), o...  2.39 us
    unnamed x10, local copies, waits for them, and re-layouts  1.49 us
  transfers between devices with their start and end apart: 7, of which 5 were waited for; matrix products, arithmetic and copies ran while one was open for 1% of the time, Pallas kernels for 0%

profile of v2, /device:TPU:0, one launch (start us, length us, event | category | flops | bytes accessed | tf_op | source)
XLA Modules:
  0.0 21.2 jit_solution(4911359964223171112)
XLA Ops:
  0.6 0.0 copy-start.2
  0.6 0.8 %constant_dynamic-update-slice_fusion.1 = bf16[1,2,64,256]{3,2,1,0:T(8,128)(2,1)S(1)} fusion(bf16[1,2,64,128]{3,2,1,0:T(8,128)(2,1)} %param.6), kind=kLoop, calls=%fused_computation.2 | loop fusion | bytes 65536
  1.4 0.0 copy-done.2
  1.4 0.0 copy-start
  1.4 4.0 %collective-permute-start.5 = (bf16[1,2,64,256]{3,2,1,0:T(8,128)(2,1)S(1)}, bf16[1,2,64,256]{3,2,1,0:T(8,128)(2,1)S(1)}, u32[]{:S(2)}, u32[]{:S(2)}) collective-permute-start(bf16[1,2,64,256]{3,2,1,0:T(8,128)(2,1)S(1)} %constant_dynamic-update-slice_fusion), channel_id=1, source_target_pairs={{0,24},{4,28},{8,16},{12,20},{16,8},{20,12},{24,0},{28,4},{1,25},{... | collective-permute-start | bytes 196616 | tf_op jit(solution)/shard_map/ppermute | solution.py:116
  5.4 0.5 %collective-permute-start.4 = (bf16[1,2,64,256]{3,2,1,0:T(8,128)(2,1)S(1)}, bf16[1,2,64,256]{3,2,1,0:T(8,128)(2,1)S(1)}, u32[]{:S(2)}, u32[]{:S(2)}) collective-permute-start(bf16[1,2,64,256]{3,2,1,0:T(8,128)(2,1)S(1)} %constant_dynamic-update-slice_fusion), channel_id=1, source_target_pairs={{0,16},{4,20},{8,24},{12,28},{16,0},{20,4},{24,8},{28,12},{1,17},{... | collective-permute-start | bytes 196616 | tf_op jit(solution)/shard_map/ppermute | solution.py:116
  5.9 0.1 collective-permute-start.3
  6.0 1.6 %collective-permute-done.5 = bf16[1,2,64,256]{3,2,1,0:T(8,128)(2,1)S(1)} collective-permute-done((bf16[1,2,64,256]{3,2,1,0:T(8,128)(2,1)S(1)}, bf16[1,2,64,256]{3,2,1,0:T(8,128)(2,1)S(1)}, u32[]{:S(2)}, u32[]{:S(2)}) %collective-permute-start.5) | collective-permute-done | bytes 65568 | tf_op jit(solution)/shard_map/ppermute | solution.py:116
  7.7 2.0 %collective-permute-done.4 = bf16[1,2,64,256]{3,2,1,0:T(8,128)(2,1)S(1)} collective-permute-done((bf16[1,2,64,256]{3,2,1,0:T(8,128)(2,1)S(1)}, bf16[1,2,64,256]{3,2,1,0:T(8,128)(2,1)S(1)}, u32[]{:S(2)}, u32[]{:S(2)}) %collective-permute-start.4) | collective-permute-done | bytes 65568 | tf_op jit(solution)/shard_map/ppermute | solution.py:116
  9.7 0.5 %collective-permute-done.3 = bf16[1,2,64,256]{3,2,1,0:T(8,128)(2,1)S(1)} collective-permute-done((bf16[1,2,64,256]{3,2,1,0:T(8,128)(2,1)S(1)}, bf16[1,2,64,256]{3,2,1,0:T(8,128)(2,1)S(1)}, u32[]{:S(2)}, u32[]{:S(2)}) %collective-permute-start.3) | collective-permute-done | bytes 65568 | tf_op jit(solution)/shard_map/ppermute | solution.py:116
  10.2 0.1 collective-permute-start.6
  10.3 0.0 copy-done
  10.4 3.7 %collective-permute-start.2 = (bf16[1,2,16,512]{3,2,1,0:T(8,128)(2,1)S(1)}, bf16[1,2,16,512]{3,2,1,0:T(8,128)(2,1)S(1)}, u32[]{:S(2)}, u32[]{:S(2)}) collective-permute-start(bf16[1,2,16,512]{3,2,1,0:T(8,128)(2,1)S(1)} %get-tuple-element.2), channel_id=1, source_target_pairs={{0,3},{1,2},{2,1},{3,0},{4,7},{5,6},{6,5},{7,4},{8,11},{9,10},{10,... | collective-permute-start | bytes 98312 | tf_op jit(solution)/shard_map/ppermute | solution.py:123
  14.0 0.0 collective-permute-start.1
  14.0 0.8 %collective-permute-start = (bf16[1,2,16,512]{3,2,1,0:T(8,128)(2,1)S(1)}, bf16[1,2,16,512]{3,2,1,0:T(8,128)(2,1)S(1)}, u32[]{:S(2)}, u32[]{:S(2)}) collective-permute-start(bf16[1,2,16,512]{3,2,1,0:T(8,128)(2,1)S(1)} %get-tuple-element.4), channel_id=1, source_target_pairs={{0,1},{1,0},{2,3},{3,2},{4,5},{5,4},{6,7},{7,6},{8,9},{9,8},{10,11... | collective-permute-start | bytes 98312 | tf_op jit(solution)/shard_map/ppermute | solution.py:123
  14.8 0.0 copy-start.3
  14.8 0.1 pad_add_fusion.meta
  14.9 0.6 %copy-done.3 = s32[8,2,4]{0,2,1:T(4,128)S(1)} copy-done((s32[8,2,4]{0,2,1:T(4,128)S(1)}, s32[8,2,4]{0,2,1:T(4,128)}, u32[]{:S(2)}) %copy-start.3) | copy-done | bytes 280
  15.5 0.1 copy.8
  15.6 0.0 copy-start.1
  15.6 0.1 reshape.7.page_slot
  15.7 0.4 %collective-permute-done.2.refs_3_ = bf16[1,2,16,512]{3,2,1,0:T(8,128)(2,1)S(1)} collective-permute-done((bf16[1,2,16,512]{3,2,1,0:T(8,128)(2,1)S(1)}, bf16[1,2,16,512]{3,2,1,0:T(8,128)(2,1)S(1)}, u32[]{:S(2)}, u32[]{:S(2)}) %collective-permute-start.2) | collective-permute-done | bytes 32800 | tf_op jit(solution)/shard_map/ppermute | solution.py:123
  16.1 2.7 %collective-permute-done.1.refs_2_ = bf16[1,2,16,512]{3,2,1,0:T(8,128)(2,1)S(1)} collective-permute-done((bf16[1,2,16,512]{3,2,1,0:T(8,128)(2,1)S(1)}, bf16[1,2,16,512]{3,2,1,0:T(8,128)(2,1)S(1)}, u32[]{:S(2)}, u32[]{:S(2)}) %collective-permute-start.1) | collective-permute-done | bytes 32800 | tf_op jit(solution)/shard_map/ppermute | solution.py:123
  18.8 0.0 collective-permute-done.refs_1_
  18.8 0.0 collective-permute-done.6.refs_5_
  18.8 0.0 copy-done.1
  18.8 2.4 %shard_map.68 = (bf16[1,2,64,512]{3,2,1,0:T(8,128)(2,1)}, bf16[16,1,16,256]{3,2,1,0:T(8,128)(2,1)}) custom-call(s32[2]{0:T(128)S(1)} %pad_add_fusion.meta, s32[3]{0:T(128)S(1)} %copy-done.1, s32[64]{0:T(128)S(1)} %reshape.7.page_slot, bf16[1,2,16,2048]{3,2,1,0:T(8,128)(2,1)S(1)} %copy-done, bf16[1,2,16,512]{3,2,1,0:T(8,128)(2,1)S(1)} %collective-permute-done.refs_1_, ...), custom_call_target="tpu_custom_call" | custom-call | tf_op jit(solution)/shard_map/pallas_call | solution.py:127
  (3 shorter events, 0.1 us)
Async XLA Ops:
  0.6 0.8 %copy-start.2 = (bf16[1,2,64,128]{3,2,1,0:T(8,128)(2,1)S(1)}, bf16[1,2,64,128]{3,2,1,0:T(8,128)(2,1)}, u32[]{:S(2)}) copy-start(bf16[1,2,64,128]{3,2,1,0:T(8,128)(2,1)} %param.7) | copy-start | bytes 98308
  1.4 8.9 %copy-start = (bf16[1,2,16,2048]{3,2,1,0:T(8,128)(2,1)S(1)}, bf16[1,2,16,2048]{3,2,1,0:T(8,128)(2,1)}, u32[]{:S(2)}) copy-start(bf16[1,2,16,2048]{3,2,1,0:T(8,128)(2,1)} %refs_0_.1) | copy-start | bytes 393220
  1.4 6.2 %collective-permute-start.5 = (bf16[1,2,64,256]{3,2,1,0:T(8,128)(2,1)S(1)}, bf16[1,2,64,256]{3,2,1,0:T(8,128)(2,1)S(1)}, u32[]{:S(2)}, u32[]{:S(2)}) collective-permute-start(bf16[1,2,64,256]{3,2,1,0:T(8,128)(2,1)S(1)} %constant_dynamic-update-slice_fusion), channel_id=1, source_target_pairs={{0,24},{4,28},{8,16},{12,20},{16,8},{20,12},{24,0},{28,4},{1,25},{... | collective-permute-start | bytes 196616 | tf_op jit(solution)/shard_map/ppermute | solution.py:116
  5.4 4.3 %collective-permute-start.4 = (bf16[1,2,64,256]{3,2,1,0:T(8,128)(2,1)S(1)}, bf16[1,2,64,256]{3,2,1,0:T(8,128)(2,1)S(1)}, u32[]{:S(2)}, u32[]{:S(2)}) collective-permute-start(bf16[1,2,64,256]{3,2,1,0:T(8,128)(2,1)S(1)} %constant_dynamic-update-slice_fusion), channel_id=1, source_target_pairs={{0,16},{4,20},{8,24},{12,28},{16,0},{20,4},{24,8},{28,12},{1,17},{... | collective-permute-start | bytes 196616 | tf_op jit(solution)/shard_map/ppermute | solution.py:116
  5.9 4.3 %collective-permute-start.3 = (bf16[1,2,64,256]{3,2,1,0:T(8,128)(2,1)S(1)}, bf16[1,2,64,256]{3,2,1,0:T(8,128)(2,1)S(1)}, u32[]{:S(2)}, u32[]{:S(2)}) collective-permute-start(bf16[1,2,64,256]{3,2,1,0:T(8,128)(2,1)S(1)} %constant_dynamic-update-slice_fusion), channel_id=1, source_target_pairs={{0,8},{4,12},{8,0},{12,4},{16,24},{20,28},{24,16},{28,20},{1,9},{5... | collective-permute-start | bytes 196616 | tf_op jit(solution)/shard_map/ppermute | solution.py:116
  10.2 8.6 %collective-permute-start.6 = (bf16[4,2,64,256]{3,2,1,0:T(8,128)(2,1)S(1)}, bf16[4,2,64,256]{3,2,1,0:T(8,128)(2,1)S(1)}, u32[]{:S(2)}, u32[]{:S(2)}) collective-permute-start(bf16[4,2,64,256]{3,2,1,0:T(8,128)(2,1)S(1)} %pad_maximum_fusion.refs_4_), channel_id=1, source_target_pairs={{0,4},{4,0},{8,12},{12,8},{16,20},{20,16},{24,28},{28,24},{1,5},{5... | collective-permute-start | bytes 786440 | tf_op jit(solution)/shard_map/ppermute | solution.py:119
  10.4 5.8 %collective-permute-start.2 = (bf16[1,2,16,512]{3,2,1,0:T(8,128)(2,1)S(1)}, bf16[1,2,16,512]{3,2,1,0:T(8,128)(2,1)S(1)}, u32[]{:S(2)}, u32[]{:S(2)}) collective-permute-start(bf16[1,2,16,512]{3,2,1,0:T(8,128)(2,1)S(1)} %get-tuple-element.2), channel_id=1, source_target_pairs={{0,3},{1,2},{2,1},{3,0},{4,7},{5,6},{6,5},{7,4},{8,11},{9,10},{10,... | collective-permute-start | bytes 98312 | tf_op jit(solution)/shard_map/ppermute | solution.py:123
  14.0 4.8 %collective-permute-start.1 = (bf16[1,2,16,512]{3,2,1,0:T(8,128)(2,1)S(1)}, bf16[1,2,16,512]{3,2,1,0:T(8,128)(2,1)S(1)}, u32[]{:S(2)}, u32[]{:S(2)}) collective-permute-start(bf16[1,2,16,512]{3,2,1,0:T(8,128)(2,1)S(1)} %get-tuple-element.3), channel_id=1, source_target_pairs={{0,2},{1,3},{2,0},{3,1},{4,6},{5,7},{6,4},{7,5},{8,10},{9,11},{10,... | collective-permute-start | bytes 98312 | tf_op jit(solution)/shard_map/ppermute | solution.py:123
  14.0 4.8 %collective-permute-start = (bf16[1,2,16,512]{3,2,1,0:T(8,128)(2,1)S(1)}, bf16[1,2,16,512]{3,2,1,0:T(8,128)(2,1)S(1)}, u32[]{:S(2)}, u32[]{:S(2)}) collective-permute-start(bf16[1,2,16,512]{3,2,1,0:T(8,128)(2,1)S(1)} %get-tuple-element.4), channel_id=1, source_target_pairs={{0,1},{1,0},{2,3},{3,2},{4,5},{5,4},{6,7},{7,6},{8,9},{9,8},{10,11... | collective-permute-start | bytes 98312 | tf_op jit(solution)/shard_map/ppermute | solution.py:123
  14.8 0.7 %copy-start.3 = (s32[8,2,4]{0,2,1:T(4,128)S(1)}, s32[8,2,4]{0,2,1:T(4,128)}, u32[]{:S(2)}) copy-start(s32[8,2,4]{0,2,1:T(4,128)} %param.9) | copy-start | bytes 772
  15.6 3.3 %copy-start.1 = (s32[3]{0:T(128)S(1)}, s32[3]{0:T(128)}, u32[]{:S(2)}) copy-start(s32[3]{0:T(128)} %doc_lengths.1) | copy-start | bytes 40

commit v3 on v2

--- a/solution.py
+++ b/solution.py
@@ -112,15 +112,17 @@
     meta = jnp.stack([my_blk, my_head]).astype(jnp.int32)
 
     pair = jnp.concatenate([key_states, value_states], axis=3)
-    near = [pair] + [
+    near = [
         lax.ppermute(pair, "blk", [(i, i ^ d) for i in range(blk_count)]) for d in range(2, blk_count, 2)
     ]
-    near = jnp.concatenate(near, axis=0)
-    far = lax.ppermute(near, "blk", [(i, i ^ 1) for i in range(blk_count)])
-    q_pieces = [query_states]
+    q_parts = []
     for d in range(1, head_count):
         part = lax.dynamic_slice_in_dim(query_states, (my_head ^ d) * width, width, axis=3)
-        q_pieces.append(lax.ppermute(part, "head", [(i, i ^ d) for i in range(head_count)]))
+        q_parts.append(lax.ppermute(part, "head", [(i, i ^ d) for i in range(head_count)]))
+    near, q_parts = lax.optimization_barrier((near, q_parts))
+    near = jnp.concatenate([pair] + near, axis=0)
+    far = lax.ppermute(near, "blk", [(i, i ^ 1) for i in range(blk_count)])
+    q_pieces = [query_states] + q_parts
 
     smem = pl.BlockSpec(memory_space=pltpu.SMEM)
     vmem = pl.BlockSpec(memory_space=pltpu.VMEM)

time: 21.4 us -> 19.3 us (0.902)
  waiting for transfers between devices: 7.29 us -> 4.24 us
  starting transfers between devices: 9.13 us -> 9.96 us
    ppermute x3, waiting for transfers between devices: 4.13 us -> 0.01 us  [per_device(): lax.ppermute(pair, 'blk', [(i, i ^ d) for i in range(blk_count)])]
    ppermute x3, starting transfers between devices: 4.45 us -> 6.34 us  [per_device(): lax.ppermute(part, 'head', [(i, i ^ d) for i in range(head_count)])]
    ppermute x3, starting transfers between devices: 4.6 us -> 3.55 us  [per_device(): lax.ppermute(pair, 'blk', [(i, i ^ d) for i in range(blk_count)])]
    dynamic_slice x1, local copies, waits for them, and re-layouts: 0.02 us -> 0.81 us  [per_device(): lax.dynamic_slice_in_dim(query_states, (my_head ^ d) * width, width, axis=3)]
    unnamed x10 -> x12, local copies, waits for them, and re-layouts: 1.49 us -> 0.71 us
    ppermute x1, waiting for transfers between devices: 0.01 us -> 0.65 us  [per_device(): far = lax.ppermute(near, 'blk', [(i, i ^ 1) for i in range(blk_count)])]
    ppermute x3, waiting for transfers between devices: 3.15 us -> 3.59 us  [per_device(): lax.ppermute(part, 'head', [(i, i ^ d) for i in range(head_count)])]
  transfers between devices with their start and end apart: 7 -> 7, of which waited for: 5 -> 2; matrix products, arithmetic and copies ran while one was open for 1% -> 1% of each run, Pallas kernels for 0% -> 0%
where the time goes in v3:
time: 19.3 us; the launch traced here: 19.1 us
  starting transfers between devices  9.96 us (52%)
  waiting for transfers between devices  4.24 us (22%)
  Pallas kernels  2.38 us (12%)
  local copies, waits for them, and re-layouts  1.63 us (8%)
  between operations  0.74 us (4%)
    ppermute x3, starting transfers between devices, per_device(): lax.ppermute(part, 'head', [(i, i ^ d) for i in range(head_count)])  6.34 us
    ppermute x3, waiting for transfers between devices, per_device(): lax.ppermute(part, 'head', [(i, i ^ d) for i in range(head_count)])  3.59 us
    ppermute x3, starting transfers between devices, per_device(): lax.ppermute(pair, 'blk', [(i, i ^ d) for i in range(blk_count)])  3.55 us
    pallas_call x1, Pallas kernels, per_device(): pl.pallas_call(functools.partial(attend_kernel, blk_count, head_count), o...  2.38 us
    dynamic_slice x1, local copies, waits for them, and re-layouts, per_device(): lax.dynamic_slice_in_dim(query_states, (my_head ^ d) * width, width, axis=3)  0.81 us
    unnamed x12, local copies, waits for them, and re-layouts  0.71 us
    ppermute x1, waiting for transfers between devices, per_device(): far = lax.ppermute(near, 'blk', [(i, i ^ 1) for i in range(blk_count)])  0.65 us
  transfers between devices with their start and end apart: 7, of which 2 were waited for; matrix products, arithmetic and copies ran while one was open for 1% of the time, Pallas kernels for 0%

profile of v3, /device:TPU:0, one launch (start us, length us, event | category | flops | bytes accessed | tf_op | source)
XLA Modules:
  0.0 19.1 jit_solution(4548434028279521294)
XLA Ops:
  0.7 0.0 copy-start.2
  0.7 0.8 %constant_dynamic-slice_fusion = (bf16[1,2,16,512]{3,2,1,0:T(8,128)(2,1)S(1)}, bf16[1,2,16,512]{3,2,1,0:T(8,128)(2,1)S(1)}, bf16[1,2,16,512]{3,2,1,0:T(8,128)(2,1)S(1)}) fusion(bf16[1,2,16,2048]{3,2,1,0:T(8,128)(2,1)} %refs_0_.1, s32[]{:T(128)S(6)} %select_n.11, s32[]{:T(128)S(6)} %select_n.10, s32[]{:T(128)S(6)} %select_n.9), kind=kLoop, calls=%fused_computation.3 | loop fusion | bytes 196620 | tf_op jit(solution)/shard_map/dynamic_slice | solution.py:120
  1.5 0.0 copy-start.3
  1.5 5.1 %collective-permute-start.5 = (bf16[1,2,16,512]{3,2,1,0:T(8,128)(2,1)S(1)}, bf16[1,2,16,512]{3,2,1,0:T(8,128)(2,1)S(1)}, u32[]{:S(2)}, u32[]{:S(2)}) collective-permute-start(bf16[1,2,16,512]{3,2,1,0:T(8,128)(2,1)S(1)} %get-tuple-element.14), channel_id=1, source_target_pairs={{0,3},{1,2},{2,1},{3,0},{4,7},{5,6},{6,5},{7,4},{8,11},{9,10},{10,... | collective-permute-start | bytes 98312 | tf_op jit(solution)/shard_map/ppermute | solution.py:121
  6.6 0.0 copy-done.2
  6.6 0.0 copy-done.3
  6.6 2.5 %collective-permute-start.2 = (bf16[1,2,64,256]{3,2,1,0:T(8,128)(2,1)S(1)}, bf16[1,2,64,256]{3,2,1,0:T(8,128)(2,1)S(1)}, u32[]{:S(2)}, u32[]{:S(2)}) collective-permute-start(bf16[1,2,64,256]{3,2,1,0:T(8,128)(2,1)S(1)} %constant_dynamic-update-slice_fusion), channel_id=1, source_target_pairs={{0,24},{4,28},{8,16},{12,20},{16,8},{20,12},{24,0},{28,4},{1,25},{... | collective-permute-start | bytes 196616 | tf_op jit(solution)/shard_map/ppermute | solution.py:116
  9.1 0.5 %collective-permute-start.1 = (bf16[1,2,64,256]{3,2,1,0:T(8,128)(2,1)S(1)}, bf16[1,2,64,256]{3,2,1,0:T(8,128)(2,1)S(1)}, u32[]{:S(2)}, u32[]{:S(2)}) collective-permute-start(bf16[1,2,64,256]{3,2,1,0:T(8,128)(2,1)S(1)} %constant_dynamic-update-slice_fusion), channel_id=1, source_target_pairs={{0,16},{4,20},{8,24},{12,28},{16,0},{20,4},{24,8},{28,12},{1,17},{... | collective-permute-start | bytes 196616 | tf_op jit(solution)/shard_map/ppermute | solution.py:116
  9.6 0.5 %collective-permute-start = (bf16[1,2,64,256]{3,2,1,0:T(8,128)(2,1)S(1)}, bf16[1,2,64,256]{3,2,1,0:T(8,128)(2,1)S(1)}, u32[]{:S(2)}, u32[]{:S(2)}) collective-permute-start(bf16[1,2,64,256]{3,2,1,0:T(8,128)(2,1)S(1)} %constant_dynamic-update-slice_fusion), channel_id=1, source_target_pairs={{0,8},{4,12},{8,0},{12,4},{16,24},{20,28},{24,16},{28,20},{1,9},{5... | collective-permute-start | bytes 196616 | tf_op jit(solution)/shard_map/ppermute | solution.py:116
  10.2 0.0 collective-permute-start.4
  10.2 0.0 collective-permute-done.5.refs_3_
  10.2 0.0 copy-start
  10.2 1.2 %collective-permute-start.3 = (bf16[1,2,16,512]{3,2,1,0:T(8,128)(2,1)S(1)}, bf16[1,2,16,512]{3,2,1,0:T(8,128)(2,1)S(1)}, u32[]{:S(2)}, u32[]{:S(2)}) collective-permute-start(bf16[1,2,16,512]{3,2,1,0:T(8,128)(2,1)S(1)} %get-tuple-element.16), channel_id=1, source_target_pairs={{0,1},{1,0},{2,3},{3,2},{4,5},{5,4},{6,7},{7,6},{8,9},{9,8},{10,11... | collective-permute-start | bytes 98312 | tf_op jit(solution)/shard_map/ppermute | solution.py:121
  11.4 3.6 %collective-permute-done.4.refs_2_ = bf16[1,2,16,512]{3,2,1,0:T(8,128)(2,1)S(1)} collective-permute-done((bf16[1,2,16,512]{3,2,1,0:T(8,128)(2,1)S(1)}, bf16[1,2,16,512]{3,2,1,0:T(8,128)(2,1)S(1)}, u32[]{:S(2)}, u32[]{:S(2)}) %collective-permute-start.4) | collective-permute-done | bytes 32800 | tf_op jit(solution)/shard_map/ppermute | solution.py:121
  15.0 0.0 collective-permute-done.3.refs_1_
  15.0 0.0 collective-permute-done.2
  15.0 0.0 collective-permute-done.1
  15.0 0.0 collective-permute-done
  15.1 0.0 copy-start.4
  15.1 0.1 collective-permute-start.6
  15.2 0.6 %copy-done.4 = s32[8,2,4]{0,2,1:T(4,128)S(1)} copy-done((s32[8,2,4]{0,2,1:T(4,128)S(1)}, s32[8,2,4]{0,2,1:T(4,128)}, u32[]{:S(2)}) %copy-start.4) | copy-done | bytes 280
  15.8 0.1 copy.8
  15.8 0.1 reshape.7.page_slot
  15.9 0.0 copy-start.1
  16.0 0.1 pad_add_fusion.meta
  16.0 0.6 %collective-permute-done.6.refs_5_ = bf16[4,2,64,256]{3,2,1,0:T(8,128)(2,1)S(1)} collective-permute-done((bf16[4,2,64,256]{3,2,1,0:T(8,128)(2,1)S(1)}, bf16[4,2,64,256]{3,2,1,0:T(8,128)(2,1)S(1)}, u32[]{:S(2)}, u32[]{:S(2)}) %collective-permute-start.6) | collective-permute-done | bytes 262176 | tf_op jit(solution)/shard_map/ppermute | solution.py:124
  16.7 0.0 copy-done
  16.7 0.0 copy-done.1
  16.7 2.4 %shard_map.68 = (bf16[1,2,64,512]{3,2,1,0:T(8,128)(2,1)}, bf16[16,1,16,256]{3,2,1,0:T(8,128)(2,1)}) custom-call(s32[2]{0:T(128)S(1)} %pad_add_fusion.meta, s32[3]{0:T(128)S(1)} %copy-done.1, s32[64]{0:T(128)S(1)} %reshape.7.page_slot, bf16[1,2,16,2048]{3,2,1,0:T(8,128)(2,1)S(1)} %copy-done, bf16[1,2,16,512]{3,2,1,0:T(8,128)(2,1)S(1)} %collective-permute-done.3.refs_1_, ...), custom_call_target="tpu_custom_call" | custom-call | tf_op jit(solution)/shard_map/pallas_call | solution.py:129
  (3 shorter events, 0.1 us)
Async XLA Ops:
  0.7 5.9 %copy-start.2 = (bf16[1,2,64,128]{3,2,1,0:T(8,128)(2,1)S(1)}, bf16[1,2,64,128]{3,2,1,0:T(8,128)(2,1)}, u32[]{:S(2)}) copy-start(bf16[1,2,64,128]{3,2,1,0:T(8,128)(2,1)} %param.6) | copy-start | bytes 98308
  1.5 5.1 %copy-start.3 = (bf16[1,2,64,128]{3,2,1,0:T(8,128)(2,1)S(1)}, bf16[1,2,64,128]{3,2,1,0:T(8,128)(2,1)}, u32[]{:S(2)}) copy-start(bf16[1,2,64,128]{3,2,1,0:T(8,128)(2,1)} %param.7) | copy-start | bytes 98308
  1.5 8.7 %collective-permute-start.5 = (bf16[1,2,16,512]{3,2,1,0:T(8,128)(2,1)S(1)}, bf16[1,2,16,512]{3,2,1,0:T(8,128)(2,1)S(1)}, u32[]{:S(2)}, u32[]{:S(2)}) collective-permute-start(bf16[1,2,16,512]{3,2,1,0:T(8,128)(2,1)S(1)} %get-tuple-element.14), channel_id=1, source_target_pairs={{0,3},{1,2},{2,1},{3,0},{4,7},{5,6},{6,5},{7,4},{8,11},{9,10},{10,... | collective-permute-start | bytes 98312 | tf_op jit(solution)/shard_map/ppermute | solution.py:121
  6.6 8.4 %collective-permute-start.2 = (bf16[1,2,64,256]{3,2,1,0:T(8,128)(2,1)S(1)}, bf16[1,2,64,256]{3,2,1,0:T(8,128)(2,1)S(1)}, u32[]{:S(2)}, u32[]{:S(2)}) collective-permute-start(bf16[1,2,64,256]{3,2,1,0:T(8,128)(2,1)S(1)} %constant_dynamic-update-slice_fusion), channel_id=1, source_target_pairs={{0,24},{4,28},{8,16},{12,20},{16,8},{20,12},{24,0},{28,4},{1,25},{... | collective-permute-start | bytes 196616 | tf_op jit(solution)/shard_map/ppermute | solution.py:116
  9.1 5.9 %collective-permute-start.1 = (bf16[1,2,64,256]{3,2,1,0:T(8,128)(2,1)S(1)}, bf16[1,2,64,256]{3,2,1,0:T(8,128)(2,1)S(1)}, u32[]{:S(2)}, u32[]{:S(2)}) collective-permute-start(bf16[1,2,64,256]{3,2,1,0:T(8,128)(2,1)S(1)} %constant_dynamic-update-slice_fusion), channel_id=1, source_target_pairs={{0,16},{4,20},{8,24},{12,28},{16,0},{20,4},{24,8},{28,12},{1,17},{... | collective-permute-start | bytes 196616 | tf_op jit(solution)/shard_map/ppermute | solution.py:116
  9.6 5.4 %collective-permute-start = (bf16[1,2,64,256]{3,2,1,0:T(8,128)(2,1)S(1)}, bf16[1,2,64,256]{3,2,1,0:T(8,128)(2,1)S(1)}, u32[]{:S(2)}, u32[]{:S(2)}) collective-permute-start(bf16[1,2,64,256]{3,2,1,0:T(8,128)(2,1)S(1)} %constant_dynamic-update-slice_fusion), channel_id=1, source_target_pairs={{0,8},{4,12},{8,0},{12,4},{16,24},{20,28},{24,16},{28,20},{1,9},{5... | collective-permute-start | bytes 196616 | tf_op jit(solution)/shard_map/ppermute | solution.py:116
  10.2 4.8 %collective-permute-start.4 = (bf16[1,2,16,512]{3,2,1,0:T(8,128)(2,1)S(1)}, bf16[1,2,16,512]{3,2,1,0:T(8,128)(2,1)S(1)}, u32[]{:S(2)}, u32[]{:S(2)}) collective-permute-start(bf16[1,2,16,512]{3,2,1,0:T(8,128)(2,1)S(1)} %get-tuple-element.15), channel_id=1, source_target_pairs={{0,2},{1,3},{2,0},{3,1},{4,6},{5,7},{6,4},{7,5},{8,10},{9,11},{10,... | collective-permute-start | bytes 98312 | tf_op jit(solution)/shard_map/ppermute | solution.py:121
  10.2 6.5 %copy-start = (bf16[1,2,16,2048]{3,2,1,0:T(8,128)(2,1)S(1)}, bf16[1,2,16,2048]{3,2,1,0:T(8,128)(2,1)}, u32[]{:S(2)}) copy-start(bf16[1,2,16,2048]{3,2,1,0:T(8,128)(2,1)} %refs_0_.1) | copy-start | bytes 393220
  10.2 4.8 %collective-permute-start.3 = (bf16[1,2,16,512]{3,2,1,0:T(8,128)(2,1)S(1)}, bf16[1,2,16,512]{3,2,1,0:T(8,128)(2,1)S(1)}, u32[]{:S(2)}, u32[]{:S(2)}) collective-permute-start(bf16[1,2,16,512]{3,2,1,0:T(8,128)(2,1)S(1)} %get-tuple-element.16), channel_id=1, source_target_pairs={{0,1},{1,0},{2,3},{3,2},{4,5},{5,4},{6,7},{7,6},{8,9},{9,8},{10,11... | collective-permute-start | bytes 98312 | tf_op jit(solution)/shard_map/ppermute | solution.py:121
  15.1 0.7 %copy-start.4 = (s32[8,2,4]{0,2,1:T(4,128)S(1)}, s32[8,2,4]{0,2,1:T(4,128)}, u32[]{:S(2)}) copy-start(s32[8,2,4]{0,2,1:T(4,128)} %param.9) | copy-start | bytes 772
  15.1 1.6 %collective-permute-start.6 = (bf16[4,2,64,256]{3,2,1,0:T(8,128)(2,1)S(1)}, bf16[4,2,64,256]{3,2,1,0:T(8,128)(2,1)S(1)}, u32[]{:S(2)}, u32[]{:S(2)}) collective-permute-start(bf16[4,2,64,256]{3,2,1,0:T(8,128)(2,1)S(1)} %pad_maximum_fusion.refs_4_), channel_id=1, source_target_pairs={{0,4},{4,0},{8,12},{12,8},{16,20},{20,16},{24,28},{28,24},{1,5},{5... | collective-permute-start | bytes 786440 | tf_op jit(solution)/shard_map/ppermute | solution.py:124
  15.9 0.7 %copy-start.1 = (s32[3]{0:T(128)S(1)}, s32[3]{0:T(128)}, u32[]{:S(2)}) copy-start(s32[3]{0:T(128)} %doc_lengths.1) | copy-start | bytes 40
